TPU v7x, 32 devices: a whole 2x2x4 slice. The times are simulated.
32 devices in a mesh: parts: 2 (over x), dp: 4 (over z), tensor: 4 (over y, core).
Axes of the slice: x: 2, y: 2, z: 4, core: 2. Of those that a mesh axis runs over, the one named last changes fastest.
Arguments:
- activations: bfloat16 [8, 128, 4096], P(('parts', 'dp'), None, 'tensor'), parts along dimension 0, may hold values from -6 to 6
- out_grad: bfloat16 [8, 128, 4096], P(('parts', 'dp'), None, 'tensor'), parts along dimension 0, may hold values from -2.5 to 2.5
- w_gate: bfloat16 [28672, 4096], P(('parts', 'dp', 'tensor')), parts along dimension 0, may hold values from -0.09375 to 0.09375
- w_up: bfloat16 [28672, 4096], P(('parts', 'dp', 'tensor')), parts along dimension 0, may hold values from -0.09375 to 0.09375
- w_down: bfloat16 [28672, 4096], P(('parts', 'dp', 'tensor')), parts along dimension 0, may hold values from -0.09375 to 0.09375
Outputs:
- fisher_gate: float32 [28672, 4096], P(('parts', 'dp', 'tensor')), parts along dimension 0
- fisher_up: float32 [28672, 4096], P(('parts', 'dp', 'tensor')), parts along dimension 0
- fisher_down: float32 [28672, 4096], P(('parts', 'dp', 'tensor')), parts along dimension 0
There are 2 independent parts, one for each index of `parts`. A program takes and returns all parts, laid end to end along the dimension named above; each array names one. Nothing has to cross between parts.
All inputs are finite; a program needn't handle non-finite values.
Results may differ from a plain program's by a relative error of at most 0.0037.
Values may be sent and summed in bfloat16 or wider, within the bound.
A program may use at most 192 MiB of HBM per device.

v0:
```python
import jax
import jax.numpy as jnp
from jax import lax
from jax.sharding import PartitionSpec as P


def example_terms(totals, x_ex, y_ex, w_gate, w_up, w_down):
    dims = (((1,), (1,)), ((), ()))
    gate_pre = lax.dot_general(w_gate, x_ex, dims, preferred_element_type=jnp.float32)
    up_pre = lax.dot_general(w_up, x_ex, dims, preferred_element_type=jnp.float32)
    sig_gate = jax.nn.sigmoid(gate_pre)
    silu_gate = gate_pre * sig_gate
    hidden = (silu_gate * up_pre).astype(jnp.bfloat16)
    grad_hidden = lax.dot_general(w_down, y_ex, dims, preferred_element_type=jnp.float32)
    grad_gate = (grad_hidden * up_pre * sig_gate * (1.0 + gate_pre * (1.0 - sig_gate))).astype(
        jnp.bfloat16
    )
    grad_up = (grad_hidden * silu_gate).astype(jnp.bfloat16)
    g_gate = jnp.dot(grad_gate, x_ex, preferred_element_type=jnp.float32)
    g_up = jnp.dot(grad_up, x_ex, preferred_element_type=jnp.float32)
    g_down = jnp.dot(hidden, y_ex, preferred_element_type=jnp.float32)
    return (totals[0] + g_gate * g_gate, totals[1] + g_up * g_up, totals[2] + g_down * g_down)


def accumulate(totals, x_rows, y_rows, w_gate, w_up, w_down):

    def step_fn(step_index, inner):
        x_ex = lax.dynamic_index_in_dim(x_rows, step_index, 0, keepdims=False)
        y_ex = lax.dynamic_index_in_dim(y_rows, step_index, 0, keepdims=False)
        return example_terms(inner, x_ex, y_ex, w_gate, w_up, w_down)

    return lax.fori_loop(0, x_rows.shape[0], step_fn, totals)


def local(activations, out_grad, w_gate, w_up, w_down):
    count = activations.shape[0] * lax.axis_size("dp")
    empty = jnp.zeros(w_gate.shape, jnp.float32)
    x_rows, y_rows = (
        lax.all_gather(activations, "dp", axis=0, tiled=True),
        lax.all_gather(out_grad, "dp", axis=0, tiled=True),
    )
    x_rows, y_rows = (
        lax.all_gather(x_rows, "tensor", axis=2, tiled=True),
        lax.all_gather(y_rows, "tensor", axis=2, tiled=True),
    )
    totals = accumulate((empty, empty, empty), x_rows, y_rows, w_gate, w_up, w_down)
    return (totals[0] / count, totals[1] / count, totals[2] / count)


def solution(mesh):
    return jax.shard_map(
        local,
        mesh=mesh,
        in_specs=(
            P(("parts", "dp"), None, "tensor"),
            P(("parts", "dp"), None, "tensor"),
            P(("parts", "dp", "tensor"), None),
            P(("parts", "dp", "tensor"), None),
            P(("parts", "dp", "tensor"), None),
        ),
        out_specs=(
            P(("parts", "dp", "tensor"), None),
            P(("parts", "dp", "tensor"), None),
            P(("parts", "dp", "tensor"), None),
        ),
        check_vma=False,
    )
```

profile of v0, /device:TPU:0, one launch (start us, length us, event | category | flops | bytes accessed | tf_op | source)
XLA Modules:
  0.0 383.6 jit_solution(17113330658727403007)
XLA Ops:
  8.7 31.5 %all-gather.9.cloned.1.call-done = bf16[4,128,1024]{2,1,0:T(8,128)(2,1)} async-done(((bf16[1,128,1024]{2,1,0:T(8,128)(2,1)}), bf16[4,128,1024]{2,1,0:T(8,128)(2,1)}) %all-gather.9.cloned.1.call-update) | async-done | bytes 1048592 | tf_op jit(solution)/shard_map/all_gather | solution.py:39
  40.3 29.0 %all-gather.5.cloned.1.call-done = bf16[4,128,1024]{2,1,0:T(8,128)(2,1)} async-done(((bf16[1,128,1024]{2,1,0:T(8,128)(2,1)}), bf16[4,128,1024]{2,1,0:T(8,128)(2,1)}) %all-gather.5.cloned.1.call-update) | async-done | bytes 1048592 | tf_op jit(solution)/shard_map/all_gather | solution.py:40
  69.3 35.5 %all-gather.11.cloned.1.call-done = bf16[4,128,4096]{2,1,0:T(8,128)(2,1)} async-done(((bf16[4,128,1024]{2,1,0:T(8,128)(2,1)}), bf16[4,128,4096]{2,1,0:T(8,128)(2,1)}) %all-gather.11.cloned.1.call-update) | async-done | bytes 4194320 | tf_op jit(solution)/shard_map/all_gather | solution.py:43
  104.8 35.9 %all-gather.7.cloned.1.call-done = bf16[4,128,4096]{2,1,0:T(8,128)(2,1)} async-done(((bf16[4,128,1024]{2,1,0:T(8,128)(2,1)}), bf16[4,128,4096]{2,1,0:T(8,128)(2,1)}) %all-gather.7.cloned.1.call-update) | async-done | bytes 4194320 | tf_op jit(solution)/shard_map/all_gather | solution.py:44
  140.8 204.2 %while.18 = (s32[]{:T(128)}, f32[896,4096]{1,0:T(8,128)}, f32[896,4096]{1,0:T(8,128)}, f32[896,4096]{1,0:T(8,128)}, bf16[4,128,4096]{2,1,0:T(8,128)(2,1)}, /*ind...) while((s32[]{:T(128)}, f32[896,4096]{1,0:T(8,128)}, ...), condition=%wide.region_1.2_spmd.clone, body=%wide.region_0.1_spmd.clone.sunk | while | flops 5672697856 | bytes 245760336 | solution.py:32
  140.8 6.0 %convolution_bitcast_fusion.6 = f32[896,128]{0,1:T(8,128)S(1)} fusion(bf16[896,4096]{1,0:T(8,128)(2,1)} %get-tuple-element.297, bf16[4,128,4096]{2,1,0:T(8,128)(2,1)} %get-tuple-element.295, s32[]{:T(128)S(6)} %copy.12), kind=kOutput, calls=%fused_computation.3.clone.1 | convolution fusion | flops 939524096 | bytes 8847364 | tf_op jit(solution)/shard_map/while/body/eval_jaxpr/dot_general | solution.py:9
  146.8 5.9 %convolution_bitcast_fusion.8 = f32[896,128]{0,1:T(8,128)S(1)} fusion(bf16[896,4096]{1,0:T(8,128)(2,1)} %get-tuple-element.296, bf16[4,128,4096]{2,1,0:T(8,128)(2,1)} %get-tuple-element.295, s32[]{:T(128)S(6)} %copy.12), kind=kOutput, calls=%fused_computation.4.clone.1 | convolution fusion | flops 939524096 | bytes 8847364 | tf_op jit(solution)/shard_map/while/body/eval_jaxpr/dot_general | solution.py:10
  152.7 3.7 convolution_bitcast_fusion.7
  156.4 9.0 %select_add_fusion.7 = f32[896,4096]{1,0:T(8,128)} fusion(f32[896,4096]{1,0:T(8,128)} %get-tuple-element.280, pred[]{:T(512)S(6)} %compare.3, bf16[4,128,4096]{2,1,0:T(8,128)(2,1)} %get-tuple-element.295, s32[]{:T(128)S(6)} %copy.12, f32[896,128]{0,1:T(8,128)S(1)} %convolution_bitcast_fusion.7, f32[896,128]{0,1:T(8,128)S(1)} %convolution_bitcast_fusion.6), kind=kOutput, calls=%fused_computation.1.clone.1 | convolution fusion | flops 951222272 | bytes 31326212 | tf_op jit(solution)/shard_map/while/body/eval_jaxpr/dot_general | solution.py:20
  165.4 9.0 %select_add_fusion.6 = f32[896,4096]{1,0:T(8,128)} fusion(f32[896,4096]{1,0:T(8,128)} %get-tuple-element.279, pred[]{:T(512)S(6)} %compare.3, bf16[4,128,4096]{2,1,0:T(8,128)(2,1)} %get-tuple-element.295, s32[]{:T(128)S(6)} %copy.12, f32[896,128]{0,1:T(8,128)S(1)} %convolution_bitcast_fusion.6, f32[896,128]{0,1:T(8,128)S(1)} %convolution_bitcast_fusion.7, ...), kind=kOutput, calls=%fused_computation.2.clone.1 | convolution fusion | flops 951681024 | bytes 31784964 | tf_op jit(solution)/shard_map/while/body/eval_jaxpr/dot_general | solution.py:19
  174.4 5.8 %select_add_fusion.8 = f32[896,4096]{1,0:T(8,128)S(1)} fusion(f32[896,4096]{1,0:T(8,128)S(1)} %bitcast.48, pred[]{:T(512)S(6)} %compare.3, bf16[4,128,4096]{2,1,0:T(8,128)(2,1)} %get-tuple-element.293, s32[]{:T(128)S(6)} %copy.12, f32[896,128]{0,1:T(8,128)S(1)} %convolution_bitcast_fusion.8, f32[896,128]{0,1:T(8,128)S(1)} %convolution_bitcast_fusion.6), kind=kOutput, calls=%fused_computation.clone.1 | convolution fusion | flops 951222272 | bytes 31326212 | tf_op jit(solution)/shard_map/while/body/eval_jaxpr/dot_general | solution.py:21
  180.2 5.2 %copy-done = f32[896,4096]{1,0:T(8,128)} copy-done((f32[896,4096]{1,0:T(8,128)}, f32[896,4096]{1,0:T(8,128)S(1)}, u32[]{:S(2)}) %copy-start) | copy-done | bytes 14680088 | tf_op jit(solution)/shard_map/while
  185.4 6.0 %convolution_bitcast_fusion.6 = f32[896,128]{0,1:T(8,128)S(1)} fusion(bf16[896,4096]{1,0:T(8,128)(2,1)} %get-tuple-element.297, bf16[4,128,4096]{2,1,0:T(8,128)(2,1)} %get-tuple-element.295, s32[]{:T(128)S(6)} %copy.12), kind=kOutput, calls=%fused_computation.3.clone.1 | convolution fusion | flops 939524096 | bytes 8847364 | tf_op jit(solution)/shard_map/while/body/eval_jaxpr/dot_general | solution.py:9
  191.4 5.9 %convolution_bitcast_fusion.8 = f32[896,128]{0,1:T(8,128)S(1)} fusion(bf16[896,4096]{1,0:T(8,128)(2,1)} %get-tuple-element.296, bf16[4,128,4096]{2,1,0:T(8,128)(2,1)} %get-tuple-element.295, s32[]{:T(128)S(6)} %copy.12), kind=kOutput, calls=%fused_computation.4.clone.1 | convolution fusion | flops 939524096 | bytes 8847364 | tf_op jit(solution)/shard_map/while/body/eval_jaxpr/dot_general | solution.py:10
  201.0 13.2 %select_add_fusion.7 = f32[896,4096]{1,0:T(8,128)} fusion(f32[896,4096]{1,0:T(8,128)} %get-tuple-element.280, pred[]{:T(512)S(6)} %compare.3, bf16[4,128,4096]{2,1,0:T(8,128)(2,1)} %get-tuple-element.295, s32[]{:T(128)S(6)} %copy.12, f32[896,128]{0,1:T(8,128)S(1)} %convolution_bitcast_fusion.7, f32[896,128]{0,1:T(8,128)S(1)} %convolution_bitcast_fusion.6), kind=kOutput, calls=%fused_computation.1.clone.1 | convolution fusion | flops 951222272 | bytes 31326212 | tf_op jit(solution)/shard_map/while/body/eval_jaxpr/dot_general | solution.py:20
  214.3 13.3 %select_add_fusion.6 = f32[896,4096]{1,0:T(8,128)} fusion(f32[896,4096]{1,0:T(8,128)} %get-tuple-element.279, pred[]{:T(512)S(6)} %compare.3, bf16[4,128,4096]{2,1,0:T(8,128)(2,1)} %get-tuple-element.295, s32[]{:T(128)S(6)} %copy.12, f32[896,128]{0,1:T(8,128)S(1)} %convolution_bitcast_fusion.6, f32[896,128]{0,1:T(8,128)S(1)} %convolution_bitcast_fusion.7, ...), kind=kOutput, calls=%fused_computation.2.clone.1 | convolution fusion | flops 951681024 | bytes 31784964 | tf_op jit(solution)/shard_map/while/body/eval_jaxpr/dot_general | solution.py:19
  227.5 5.8 %select_add_fusion.8 = f32[896,4096]{1,0:T(8,128)S(1)} fusion(f32[896,4096]{1,0:T(8,128)S(1)} %bitcast.48, pred[]{:T(512)S(6)} %compare.3, bf16[4,128,4096]{2,1,0:T(8,128)(2,1)} %get-tuple-element.293, s32[]{:T(128)S(6)} %copy.12, f32[896,128]{0,1:T(8,128)S(1)} %convolution_bitcast_fusion.8, f32[896,128]{0,1:T(8,128)S(1)} %convolution_bitcast_fusion.6), kind=kOutput, calls=%fused_computation.clone.1 | convolution fusion | flops 951222272 | bytes 31326212 | tf_op jit(solution)/shard_map/while/body/eval_jaxpr/dot_general | solution.py:21
  233.4 5.2 %copy-done = f32[896,4096]{1,0:T(8,128)} copy-done((f32[896,4096]{1,0:T(8,128)}, f32[896,4096]{1,0:T(8,128)S(1)}, u32[]{:S(2)}) %copy-start) | copy-done | bytes 14680088 | tf_op jit(solution)/shard_map/while
  238.6 6.0 %convolution_bitcast_fusion.6 = f32[896,128]{0,1:T(8,128)S(1)} fusion(bf16[896,4096]{1,0:T(8,128)(2,1)} %get-tuple-element.297, bf16[4,128,4096]{2,1,0:T(8,128)(2,1)} %get-tuple-element.295, s32[]{:T(128)S(6)} %copy.12), kind=kOutput, calls=%fused_computation.3.clone.1 | convolution fusion | flops 939524096 | bytes 8847364 | tf_op jit(solution)/shard_map/while/body/eval_jaxpr/dot_general | solution.py:9
  244.6 5.9 %convolution_bitcast_fusion.8 = f32[896,128]{0,1:T(8,128)S(1)} fusion(bf16[896,4096]{1,0:T(8,128)(2,1)} %get-tuple-element.296, bf16[4,128,4096]{2,1,0:T(8,128)(2,1)} %get-tuple-element.295, s32[]{:T(128)S(6)} %copy.12), kind=kOutput, calls=%fused_computation.4.clone.1 | convolution fusion | flops 939524096 | bytes 8847364 | tf_op jit(solution)/shard_map/while/body/eval_jaxpr/dot_general | solution.py:10
  254.2 13.2 %select_add_fusion.7 = f32[896,4096]{1,0:T(8,128)} fusion(f32[896,4096]{1,0:T(8,128)} %get-tuple-element.280, pred[]{:T(512)S(6)} %compare.3, bf16[4,128,4096]{2,1,0:T(8,128)(2,1)} %get-tuple-element.295, s32[]{:T(128)S(6)} %copy.12, f32[896,128]{0,1:T(8,128)S(1)} %convolution_bitcast_fusion.7, f32[896,128]{0,1:T(8,128)S(1)} %convolution_bitcast_fusion.6), kind=kOutput, calls=%fused_computation.1.clone.1 | convolution fusion | flops 951222272 | bytes 31326212 | tf_op jit(solution)/shard_map/while/body/eval_jaxpr/dot_general | solution.py:20
  267.4 13.3 %select_add_fusion.6 = f32[896,4096]{1,0:T(8,128)} fusion(f32[896,4096]{1,0:T(8,128)} %get-tuple-element.279, pred[]{:T(512)S(6)} %compare.3, bf16[4,128,4096]{2,1,0:T(8,128)(2,1)} %get-tuple-element.295, s32[]{:T(128)S(6)} %copy.12, f32[896,128]{0,1:T(8,128)S(1)} %convolution_bitcast_fusion.6, f32[896,128]{0,1:T(8,128)S(1)} %convolution_bitcast_fusion.7, ...), kind=kOutput, calls=%fused_computation.2.clone.1 | convolution fusion | flops 951681024 | bytes 31784964 | tf_op jit(solution)/shard_map/while/body/eval_jaxpr/dot_general | solution.py:19
  280.7 5.8 %select_add_fusion.8 = f32[896,4096]{1,0:T(8,128)S(1)} fusion(f32[896,4096]{1,0:T(8,128)S(1)} %bitcast.48, pred[]{:T(512)S(6)} %compare.3, bf16[4,128,4096]{2,1,0:T(8,128)(2,1)} %get-tuple-element.293, s32[]{:T(128)S(6)} %copy.12, f32[896,128]{0,1:T(8,128)S(1)} %convolution_bitcast_fusion.8, f32[896,128]{0,1:T(8,128)S(1)} %convolution_bitcast_fusion.6), kind=kOutput, calls=%fused_computation.clone.1 | convolution fusion | flops 951222272 | bytes 31326212 | tf_op jit(solution)/shard_map/while/body/eval_jaxpr/dot_general | solution.py:21
  286.6 5.2 %copy-done = f32[896,4096]{1,0:T(8,128)} copy-done((f32[896,4096]{1,0:T(8,128)}, f32[896,4096]{1,0:T(8,128)S(1)}, u32[]{:S(2)}) %copy-start) | copy-done | bytes 14680088 | tf_op jit(solution)/shard_map/while
  291.8 6.0 %convolution_bitcast_fusion.6 = f32[896,128]{0,1:T(8,128)S(1)} fusion(bf16[896,4096]{1,0:T(8,128)(2,1)} %get-tuple-element.297, bf16[4,128,4096]{2,1,0:T(8,128)(2,1)} %get-tuple-element.295, s32[]{:T(128)S(6)} %copy.12), kind=kOutput, calls=%fused_computation.3.clone.1 | convolution fusion | flops 939524096 | bytes 8847364 | tf_op jit(solution)/shard_map/while/body/eval_jaxpr/dot_general | solution.py:9
  297.8 5.9 %convolution_bitcast_fusion.8 = f32[896,128]{0,1:T(8,128)S(1)} fusion(bf16[896,4096]{1,0:T(8,128)(2,1)} %get-tuple-element.296, bf16[4,128,4096]{2,1,0:T(8,128)(2,1)} %get-tuple-element.295, s32[]{:T(128)S(6)} %copy.12), kind=kOutput, calls=%fused_computation.4.clone.1 | convolution fusion | flops 939524096 | bytes 8847364 | tf_op jit(solution)/shard_map/while/body/eval_jaxpr/dot_general | solution.py:10
  307.3 13.2 %select_add_fusion.7 = f32[896,4096]{1,0:T(8,128)} fusion(f32[896,4096]{1,0:T(8,128)} %get-tuple-element.280, pred[]{:T(512)S(6)} %compare.3, bf16[4,128,4096]{2,1,0:T(8,128)(2,1)} %get-tuple-element.295, s32[]{:T(128)S(6)} %copy.12, f32[896,128]{0,1:T(8,128)S(1)} %convolution_bitcast_fusion.7, f32[896,128]{0,1:T(8,128)S(1)} %convolution_bitcast_fusion.6), kind=kOutput, calls=%fused_computation.1.clone.1 | convolution fusion | flops 951222272 | bytes 31326212 | tf_op jit(solution)/shard_map/while/body/eval_jaxpr/dot_general | solution.py:20
  320.6 13.3 %select_add_fusion.6 = f32[896,4096]{1,0:T(8,128)} fusion(f32[896,4096]{1,0:T(8,128)} %get-tuple-element.279, pred[]{:T(512)S(6)} %compare.3, bf16[4,128,4096]{2,1,0:T(8,128)(2,1)} %get-tuple-element.295, s32[]{:T(128)S(6)} %copy.12, f32[896,128]{0,1:T(8,128)S(1)} %convolution_bitcast_fusion.6, f32[896,128]{0,1:T(8,128)S(1)} %convolution_bitcast_fusion.7, ...), kind=kOutput, calls=%fused_computation.2.clone.1 | convolution fusion | flops 951681024 | bytes 31784964 | tf_op jit(solution)/shard_map/while/body/eval_jaxpr/dot_general | solution.py:19
  333.9 5.8 %select_add_fusion.8 = f32[896,4096]{1,0:T(8,128)S(1)} fusion(f32[896,4096]{1,0:T(8,128)S(1)} %bitcast.48, pred[]{:T(512)S(6)} %compare.3, bf16[4,128,4096]{2,1,0:T(8,128)(2,1)} %get-tuple-element.293, s32[]{:T(128)S(6)} %copy.12, f32[896,128]{0,1:T(8,128)S(1)} %convolution_bitcast_fusion.8, f32[896,128]{0,1:T(8,128)S(1)} %convolution_bitcast_fusion.6), kind=kOutput, calls=%fused_computation.clone.1 | convolution fusion | flops 951222272 | bytes 31326212 | tf_op jit(solution)/shard_map/while/body/eval_jaxpr/dot_general | solution.py:21
  339.7 5.2 %copy-done = f32[896,4096]{1,0:T(8,128)} copy-done((f32[896,4096]{1,0:T(8,128)}, f32[896,4096]{1,0:T(8,128)S(1)}, u32[]{:S(2)}) %copy-start) | copy-done | bytes 14680088 | tf_op jit(solution)/shard_map/while
  344.9 13.4 %broadcast_multiply_fusion.2 = f32[896,4096]{1,0:T(8,128)} fusion(f32[896,4096]{1,0:T(8,128)} %get-tuple-element.159), kind=kLoop, calls=%fused_computation.35 | loop fusion | flops 3670016 | bytes 29360128 | tf_op jit(solution)/shard_map/div | solution.py:47
  358.3 18.8 %broadcast_multiply_fusion = (f32[896,4096]{1,0:T(8,128)}, f32[896,4096]{1,0:T(8,128)}) fusion(f32[896,4096]{1,0:T(8,128)} %get-tuple-element.161, f32[896,4096]{1,0:T(8,128)} %get-tuple-element.160), kind=kLoop, calls=%fused_computation.33 | loop fusion | flops 7340032 | bytes 58720256 | tf_op jit(solution)/shard_map/div | solution.py:47
  (74 shorter events, 12.7 us)
Async XLA Ops:
  7.2 33.1 %all-gather.9.cloned.1.call-start = ((), (), s32[]{:S(2)}) async-start(), calls=%async_computation.2 | async-start | bytes 1310720 | tf_op jit(solution)/shard_map/all_gather | solution.py:39
  7.9 61.4 %all-gather.5.cloned.1.call-start = ((), (), s32[]{:S(2)}) async-start(), calls=%async_computation | async-start | bytes 1310720 | tf_op jit(solution)/shard_map/all_gather | solution.py:40
  8.6 96.2 %all-gather.11.cloned.1.call-start = ((), (), s32[]{:S(2)}) async-start(), calls=%async_computation.3 | async-start | bytes 5242880 | tf_op jit(solution)/shard_map/all_gather | solution.py:43
  40.3 100.5 %all-gather.7.cloned.1.call-start = ((), (), s32[]{:S(2)}) async-start(), calls=%async_computation.1 | async-start | bytes 5242880 | tf_op jit(solution)/shard_map/all_gather | solution.py:44
  140.8 11.9 %slice-start.4 = ((s8[7340032]{0:T(1024)(128)(4,1)}), s8[3145728]{0:T(1024)(128)(4,1)S(1)}, s32[]{:S(2)}) async-start(s8[7340032]{0:T(1024)(128)(4,1)} %bitcast.49), calls=%async_computation.8 | async-start | bytes 6291456 | tf_op jit(solution)/shard_map/while
  140.8 11.9 %slice-start.5 = ((s8[7340032]{0:T(1024)(128)(4,1)}), s8[4194304]{0:T(1024)(128)(4,1)S(1)}, s32[]{:S(2)}) async-start(s8[7340032]{0:T(1024)(128)(4,1)} %bitcast.49), calls=%async_computation.9 | async-start | bytes 8388608 | tf_op jit(solution)/shard_map/while
  156.3 18.0 %slice-start = ((s8[14680064]{0:T(1024)(128)(4,1)}), s8[4194304]{0:T(1024)(128)(4,1)S(1)}, s32[]{:S(2)}) async-start(s8[14680064]{0:T(1024)(128)(4,1)} %bitcast.47), calls=%async_computation.4 | async-start | bytes 8388608 | tf_op jit(solution)/shard_map/while
  156.4 18.0 %slice-start.1 = ((s8[14680064]{0:T(1024)(128)(4,1)}), s8[4194304]{0:T(1024)(128)(4,1)S(1)}, s32[]{:S(2)}) async-start(s8[14680064]{0:T(1024)(128)(4,1)} %bitcast.47), calls=%async_computation.5 | async-start | bytes 8388608 | tf_op jit(solution)/shard_map/while
  165.4 9.0 %slice-start.2 = ((s8[14680064]{0:T(1024)(128)(4,1)}), s8[4194304]{0:T(1024)(128)(4,1)S(1)}, s32[]{:S(2)}) async-start(s8[14680064]{0:T(1024)(128)(4,1)} %bitcast.47), calls=%async_computation.6 | async-start | bytes 8388608 | tf_op jit(solution)/shard_map/while
  165.4 9.0 %slice-start.3 = ((s8[14680064]{0:T(1024)(128)(4,1)}), s8[2097152]{0:T(1024)(128)(4,1)S(1)}, s32[]{:S(2)}) async-start(s8[14680064]{0:T(1024)(128)(4,1)} %bitcast.47), calls=%async_computation.7 | async-start | bytes 4194304 | tf_op jit(solution)/shard_map/while
  180.2 5.2 %copy-start = (f32[896,4096]{1,0:T(8,128)}, f32[896,4096]{1,0:T(8,128)S(1)}, u32[]{:S(2)}) copy-start(f32[896,4096]{1,0:T(8,128)S(1)} %select_add_fusion.8) | copy-start | bytes 44040196 | tf_op jit(solution)/shard_map/while
  185.4 11.9 %slice-start.4 = ((s8[7340032]{0:T(1024)(128)(4,1)}), s8[3145728]{0:T(1024)(128)(4,1)S(1)}, s32[]{:S(2)}) async-start(s8[7340032]{0:T(1024)(128)(4,1)} %bitcast.49), calls=%async_computation.8 | async-start | bytes 6291456 | tf_op jit(solution)/shard_map/while
  185.4 11.9 %slice-start.5 = ((s8[7340032]{0:T(1024)(128)(4,1)}), s8[4194304]{0:T(1024)(128)(4,1)S(1)}, s32[]{:S(2)}) async-start(s8[7340032]{0:T(1024)(128)(4,1)} %bitcast.49), calls=%async_computation.9 | async-start | bytes 8388608 | tf_op jit(solution)/shard_map/while
  201.0 26.5 %slice-start = ((s8[14680064]{0:T(1024)(128)(4,1)}), s8[4194304]{0:T(1024)(128)(4,1)S(1)}, s32[]{:S(2)}) async-start(s8[14680064]{0:T(1024)(128)(4,1)} %bitcast.47), calls=%async_computation.4 | async-start | bytes 8388608 | tf_op jit(solution)/shard_map/while
  201.0 26.5 %slice-start.1 = ((s8[14680064]{0:T(1024)(128)(4,1)}), s8[4194304]{0:T(1024)(128)(4,1)S(1)}, s32[]{:S(2)}) async-start(s8[14680064]{0:T(1024)(128)(4,1)} %bitcast.47), calls=%async_computation.5 | async-start | bytes 8388608 | tf_op jit(solution)/shard_map/while
  214.3 13.3 %slice-start.2 = ((s8[14680064]{0:T(1024)(128)(4,1)}), s8[4194304]{0:T(1024)(128)(4,1)S(1)}, s32[]{:S(2)}) async-start(s8[14680064]{0:T(1024)(128)(4,1)} %bitcast.47), calls=%async_computation.6 | async-start | bytes 8388608 | tf_op jit(solution)/shard_map/while
  214.3 13.3 %slice-start.3 = ((s8[14680064]{0:T(1024)(128)(4,1)}), s8[2097152]{0:T(1024)(128)(4,1)S(1)}, s32[]{:S(2)}) async-start(s8[14680064]{0:T(1024)(128)(4,1)} %bitcast.47), calls=%async_computation.7 | async-start | bytes 4194304 | tf_op jit(solution)/shard_map/while
  233.4 5.2 %copy-start = (f32[896,4096]{1,0:T(8,128)}, f32[896,4096]{1,0:T(8,128)S(1)}, u32[]{:S(2)}) copy-start(f32[896,4096]{1,0:T(8,128)S(1)} %select_add_fusion.8) | copy-start | bytes 44040196 | tf_op jit(solution)/shard_map/while
  238.6 11.9 %slice-start.4 = ((s8[7340032]{0:T(1024)(128)(4,1)}), s8[3145728]{0:T(1024)(128)(4,1)S(1)}, s32[]{:S(2)}) async-start(s8[7340032]{0:T(1024)(128)(4,1)} %bitcast.49), calls=%async_computation.8 | async-start | bytes 6291456 | tf_op jit(solution)/shard_map/while
  238.6 11.9 %slice-start.5 = ((s8[7340032]{0:T(1024)(128)(4,1)}), s8[4194304]{0:T(1024)(128)(4,1)S(1)}, s32[]{:S(2)}) async-start(s8[7340032]{0:T(1024)(128)(4,1)} %bitcast.49), calls=%async_computation.9 | async-start | bytes 8388608 | tf_op jit(solution)/shard_map/while
  254.2 26.5 %slice-start = ((s8[14680064]{0:T(1024)(128)(4,1)}), s8[4194304]{0:T(1024)(128)(4,1)S(1)}, s32[]{:S(2)}) async-start(s8[14680064]{0:T(1024)(128)(4,1)} %bitcast.47), calls=%async_computation.4 | async-start | bytes 8388608 | tf_op jit(solution)/shard_map/while
  254.2 26.5 %slice-start.1 = ((s8[14680064]{0:T(1024)(128)(4,1)}), s8[4194304]{0:T(1024)(128)(4,1)S(1)}, s32[]{:S(2)}) async-start(s8[14680064]{0:T(1024)(128)(4,1)} %bitcast.47), calls=%async_computation.5 | async-start | bytes 8388608 | tf_op jit(solution)/shard_map/while
  267.4 13.3 %slice-start.2 = ((s8[14680064]{0:T(1024)(128)(4,1)}), s8[4194304]{0:T(1024)(128)(4,1)S(1)}, s32[]{:S(2)}) async-start(s8[14680064]{0:T(1024)(128)(4,1)} %bitcast.47), calls=%async_computation.6 | async-start | bytes 8388608 | tf_op jit(solution)/shard_map/while
  267.4 13.3 %slice-start.3 = ((s8[14680064]{0:T(1024)(128)(4,1)}), s8[2097152]{0:T(1024)(128)(4,1)S(1)}, s32[]{:S(2)}) async-start(s8[14680064]{0:T(1024)(128)(4,1)} %bitcast.47), calls=%async_computation.7 | async-start | bytes 4194304 | tf_op jit(solution)/shard_map/while
  286.5 5.2 %copy-start = (f32[896,4096]{1,0:T(8,128)}, f32[896,4096]{1,0:T(8,128)S(1)}, u32[]{:S(2)}) copy-start(f32[896,4096]{1,0:T(8,128)S(1)} %select_add_fusion.8) | copy-start | bytes 44040196 | tf_op jit(solution)/shard_map/while
  291.8 11.9 %slice-start.4 = ((s8[7340032]{0:T(1024)(128)(4,1)}), s8[3145728]{0:T(1024)(128)(4,1)S(1)}, s32[]{:S(2)}) async-start(s8[7340032]{0:T(1024)(128)(4,1)} %bitcast.49), calls=%async_computation.8 | async-start | bytes 6291456 | tf_op jit(solution)/shard_map/while
  291.8 11.9 %slice-start.5 = ((s8[7340032]{0:T(1024)(128)(4,1)}), s8[4194304]{0:T(1024)(128)(4,1)S(1)}, s32[]{:S(2)}) async-start(s8[7340032]{0:T(1024)(128)(4,1)} %bitcast.49), calls=%async_computation.9 | async-start | bytes 8388608 | tf_op jit(solution)/shard_map/while
  307.3 26.5 %slice-start = ((s8[14680064]{0:T(1024)(128)(4,1)}), s8[4194304]{0:T(1024)(128)(4,1)S(1)}, s32[]{:S(2)}) async-start(s8[14680064]{0:T(1024)(128)(4,1)} %bitcast.47), calls=%async_computation.4 | async-start | bytes 8388608 | tf_op jit(solution)/shard_map/while
  307.3 26.5 %slice-start.1 = ((s8[14680064]{0:T(1024)(128)(4,1)}), s8[4194304]{0:T(1024)(128)(4,1)S(1)}, s32[]{:S(2)}) async-start(s8[14680064]{0:T(1024)(128)(4,1)} %bitcast.47), calls=%async_computation.5 | async-start | bytes 8388608 | tf_op jit(solution)/shard_map/while
  320.6 13.3 %slice-start.2 = ((s8[14680064]{0:T(1024)(128)(4,1)}), s8[4194304]{0:T(1024)(128)(4,1)S(1)}, s32[]{:S(2)}) async-start(s8[14680064]{0:T(1024)(128)(4,1)} %bitcast.47), calls=%async_computation.6 | async-start | bytes 8388608 | tf_op jit(solution)/shard_map/while
  320.6 13.3 %slice-start.3 = ((s8[14680064]{0:T(1024)(128)(4,1)}), s8[2097152]{0:T(1024)(128)(4,1)S(1)}, s32[]{:S(2)}) async-start(s8[14680064]{0:T(1024)(128)(4,1)} %bitcast.47), calls=%async_computation.7 | async-start | bytes 4194304 | tf_op jit(solution)/shard_map/while
  339.7 5.2 %copy-start = (f32[896,4096]{1,0:T(8,128)}, f32[896,4096]{1,0:T(8,128)S(1)}, u32[]{:S(2)}) copy-start(f32[896,4096]{1,0:T(8,128)S(1)} %select_add_fusion.8) | copy-start | bytes 44040196 | tf_op jit(solution)/shard_map/while
Sparse Core Ops, SparseCore 0:
  9.6 30.6 all-gather.8
  41.8 27.4 all-gather.4
  70.8 33.9 all-gather.10
  106.3 34.4 all-gather.6
where the time goes:
time: 384 us
  matrix products  183 us (48%)
  waiting for transfers between devices  133 us (35%)
  other arithmetic  32.2 us (8%)
  local copies, waits for them, and re-layouts  20.9 us (5%)
  between operations  13.8 us (4%)
    dot_general x4, matrix products, example_terms(): g_gate = jnp.dot(grad_gate, x_ex, preferred_element_type=jnp.float32)  48.7 us
    dot_general x4, matrix products, example_terms(): g_up = jnp.dot(grad_up, x_ex, preferred_element_type=jnp.float32)  48.7 us
    all_gather x1, waiting for transfers between devices, local(): lax.all_gather(y_rows, 'tensor', axis=2, tiled=True)  35.9 us
    all_gather x1, waiting for transfers between devices, local(): lax.all_gather(x_rows, 'tensor', axis=2, tiled=True)  35.5 us
    div x2, other arithmetic, local(): return (totals[0] / count, totals[1] / count, totals[2] / count)  32.2 us
    all_gather x1, waiting for transfers between devices, local(): lax.all_gather(activations, 'dp', axis=0, tiled=True)  31.5 us
    all_gather x1, waiting for transfers between devices, local(): lax.all_gather(out_grad, 'dp', axis=0, tiled=True)  29 us
    dot_general x4, matrix products, example_terms(): lax.dot_general(w_gate, x_ex, dims, preferred_element_type=jnp.float32)  23.9 us
  transfers between devices with their start and end apart: 4, of which 4 were waited for; matrix products, arithmetic and copies ran while one was open for 0% of the time, Pallas kernels for 0%

commit v1 on v0

v1 whole, which is shorter than its diff:
```python
import functools

import jax
import jax.numpy as jnp
from jax import lax
from jax.experimental import pallas as pl
from jax.experimental.pallas import tpu as pltpu
from jax.sharding import PartitionSpec as P

MESH = pl.DeviceIdType.MESH
NT = (((1,), (1,)), ((), ()))


def row_chunk(rows, most):
    return max(r for r in range(16, most + 1, 16) if rows % r == 0)


def gather_forward(
    n_dp, n_tensor,
    x_ref, y_ref, wg_ref, wu_ref, wd_ref,
    xo_ref, yo_ref, gg_ref, gu_ref, hid_ref,
    xb, yb, wg, wu, wd, gate, up,
    own_sem, w_sem, recv_sem, line_sem, sib_sem, out_sem,
):
    z, t = lax.axis_index("dp"), lax.axis_index("tensor")
    core = lax.rem(t, 2)
    line = t // 2
    n_lines = n_tensor // 2
    unit = x_ref.shape[0]
    depth = x_ref.shape[1]
    rows = wg.shape[0]
    bufs = (xb, yb)

    weights = [
        pltpu.make_async_copy(src, dst, w_sem.at[i])
        for i, (src, dst) in enumerate(((wg_ref, wg), (wu_ref, wu), (wd_ref, wd)))
    ]
    own = [
        pltpu.make_async_copy(
            src, bufs[a].at[t, pl.ds(z * unit, unit), :], own_sem.at[a]
        )
        for a, src in enumerate((x_ref, y_ref))
    ]
    for copy in own:
        copy.start()

    barrier = pltpu.get_barrier_semaphore()
    has_up, has_down = z < n_dp - 1, z > 0

    @pl.when(has_up)
    def _():
        pl.semaphore_signal(barrier, 1, device_id={"dp": z + 1}, device_id_type=MESH)

    @pl.when(has_down)
    def _():
        pl.semaphore_signal(barrier, 1, device_id={"dp": z - 1}, device_id_type=MESH)

    def peer(j):
        return lax.rem(line + j, n_lines) * 2 + core

    for j in range(1, n_lines):
        pl.semaphore_signal(barrier, 1, device_id={"tensor": peer(j)}, device_id_type=MESH)
    sibling = line * 2 + 1 - core
    pl.semaphore_signal(barrier, 1, device_id={"tensor": sibling}, device_id_type=MESH)
    pl.semaphore_wait(
        barrier, n_lines + has_up.astype(jnp.int32) + has_down.astype(jnp.int32)
    )
    for copy in own:
        copy.wait()

    sent = []

    def slot(a, zz, tt):
        return bufs[a].at[tt, pl.ds(zz * unit, unit), :]

    def push(a, zz, tt, sem, target, cond):
        copy = pltpu.make_async_remote_copy(
            src_ref=slot(a, zz, tt),
            dst_ref=slot(a, zz, tt),
            send_sem=sem,
            recv_sem=recv_sem.at[a, zz, tt],
            device_id=target,
            device_id_type=MESH,
        )
        if cond is None:
            copy.start()
            sent.append(copy.wait_send)
        else:
            pl.when(cond)(copy.start)
            sent.append(lambda: pl.when(cond)(copy.wait_send))

    def arrived(a, zz, tt):
        pltpu.make_async_copy(slot(a, zz, tt), slot(a, zz, tt), recv_sem.at[a, zz, tt]).wait()

    def guarded(cond, do):
        if cond is None:
            do()
        else:
            pl.when(cond)(do)

    def both(*conds):
        conds = [c for c in conds if c is not None]
        return functools.reduce(jnp.logical_and, conds) if conds else None

    def on_line(a, k):
        for sign in (1, -1) if k else (0,):
            zz = z - sign * k
            cond = None if k == 0 else (zz >= 0 if sign > 0 else zz < n_dp)
            safe = jnp.clip(zz, 0, n_dp - 1)
            if k:
                guarded(cond, lambda: arrived(a, safe, t))
            if sign >= 0:
                push(a, safe, t, line_sem.at[a, safe, 0], {"dp": z + 1}, both(cond, has_up))
            if sign <= 0:
                push(a, safe, t, line_sem.at[a, safe, 1], {"dp": z - 1}, both(cond, has_down))
            for j in range(1, n_lines):
                push(a, safe, t, line_sem.at[a, safe, 1 + j], {"tensor": peer(j)}, cond)
            push(a, safe, t, sib_sem.at[a, safe, line], {"tensor": sibling}, cond)

    def from_peers(a, k):
        for sign in (1, -1) if k else (0,):
            zz = z - sign * k
            cond = None if k == 0 else (zz >= 0 if sign > 0 else zz < n_dp)
            safe = jnp.clip(zz, 0, n_dp - 1)
            for j in range(1, n_lines):
                tt = peer(j)
                guarded(cond, lambda: arrived(a, safe, tt))
                push(a, safe, tt, sib_sem.at[a, safe, tt // 2], {"tensor": sibling}, cond)

    def from_sibling(a):
        for zz in range(n_dp):
            for l in range(n_lines):
                arrived(a, zz, 2 * l + 1 - core)

    chunk = row_chunk(rows, 448)

    def project(w, act, acc, k):
        @pl.loop(0, rows // chunk)
        def _(i):
            r = pl.ds(pl.multiple_of(i * chunk, chunk), chunk)
            part = lax.dot_general(
                w[r, k * depth:(k + 1) * depth], act[k], NT,
                preferred_element_type=jnp.float32,
            )
            if k == 0:
                acc[r, :] = part
            else:
                acc[r, :] += part

    on_line(0, 0)
    for copy in weights:
        copy.start()
    half = max(1, n_dp // 2)
    for k in range(1, n_dp):
        if k == half:
            on_line(1, 0)
        on_line(0, k)
        from_peers(0, k - 1)
    if n_dp == 1:
        on_line(1, 0)
    from_peers(0, n_dp - 1)
    on_line(1, 1)
    from_sibling(0)
    x_out = pltpu.make_async_copy(xb, xo_ref, out_sem.at[0])
    x_out.start()
    weights[0].wait()
    weights[1].wait()
    steps = [(w, acc, k) for k in range(n_tensor) for w, acc in ((wg, gate), (wu, up))]
    done = 0
    for k in range(2, n_dp):
        upto = len(steps) * (k - 1) // (n_dp - 2)
        for w, acc, kk in steps[done:upto]:
            project(w, xb, acc, kk)
        done = upto
        on_line(1, k)
        from_peers(1, k - 2)
    for w, acc, kk in steps[done:]:
        project(w, xb, acc, kk)

    small = row_chunk(rows, 64)

    @pl.loop(0, rows // small)
    def _(i):
        r = pl.ds(pl.multiple_of(i * small, small), small)
        g, u = gate[r, :], up[r, :]
        sig = jax.nn.sigmoid(g)
        silu = g * sig
        hid_ref[r, :] = (silu * u).astype(jnp.bfloat16)
        gate[r, :] = u * sig * (1.0 + g * (1.0 - sig))
        up[r, :] = silu

    from_peers(1, n_dp - 2)
    from_peers(1, n_dp - 1)
    from_sibling(1)
    y_out = pltpu.make_async_copy(yb, yo_ref, out_sem.at[1])
    y_out.start()
    weights[2].wait()

    width = n_tensor

    @pl.loop(0, rows // chunk)
    def _(i):
        r = pl.ds(pl.multiple_of(i * chunk, chunk), chunk)
        grad = lax.dot_general(wd[r, :depth], yb[0], NT, preferred_element_type=jnp.float32)
        for k in range(1, width):
            grad += lax.dot_general(
                wd[r, k * depth:(k + 1) * depth], yb[k], NT,
                preferred_element_type=jnp.float32,
            )
        gg_ref[r, :] = (grad * gate[r, :]).astype(jnp.bfloat16)
        gu_ref[r, :] = (grad * up[r, :]).astype(jnp.bfloat16)

    for wait in sent:
        wait()
    x_out.wait()
    y_out.wait()


def squares(count, seq, gg_ref, gu_ref, hid_ref, x_ref, y_ref, fg_ref, fu_ref, fd_ref):
    rows, columns = fg_ref.shape
    chunk = row_chunk(rows, 448)
    wide = 256 if columns % 256 == 0 else columns
    for act, grads, out in ((x_ref, gg_ref, fg_ref), (x_ref, gu_ref, fu_ref), (y_ref, hid_ref, fd_ref)):
        for q in range(columns // wide):
            @pl.loop(0, rows // chunk)
            def _(i):
                r = pl.ds(pl.multiple_of(i * chunk, chunk), chunk)
                total = None
                for e in range(count):
                    span = slice(e * seq, (e + 1) * seq)
                    g = jnp.dot(
                        grads[r, span], act[span, q * wide:(q + 1) * wide],
                        preferred_element_type=jnp.float32,
                    )
                    total = g * g if total is None else total + g * g
                out[r, q * wide:(q + 1) * wide] = total * (1.0 / count)


def local(n_dp, n_tensor, activations, out_grad, w_gate, w_up, w_down):
    per, seq, depth = activations.shape
    count = per * n_dp
    rows, features = w_gate.shape
    tokens = count * seq
    x = activations.reshape(per * seq, depth)
    y = out_grad.reshape(per * seq, depth)
    n_lines = n_tensor // 2
    blocks = jax.ShapeDtypeStruct((n_tensor, tokens, depth), jnp.bfloat16)
    grads = jax.ShapeDtypeStruct((rows, tokens), jnp.bfloat16)
    anywhere = pl.BlockSpec(memory_space=pl.ANY)
    in_vmem = pl.BlockSpec(memory_space=pltpu.VMEM)
    xb, yb, gg, gu, hid = pl.pallas_call(
        functools.partial(gather_forward, n_dp, n_tensor),
        out_shape=(blocks, blocks, grads, grads, grads),
        in_specs=[anywhere] * 5,
        out_specs=(anywhere, anywhere, in_vmem, in_vmem, in_vmem),
        scratch_shapes=[
            pltpu.VMEM(blocks.shape, jnp.bfloat16),
            pltpu.VMEM(blocks.shape, jnp.bfloat16),
            pltpu.VMEM((rows, features), jnp.bfloat16),
            pltpu.VMEM((rows, features), jnp.bfloat16),
            pltpu.VMEM((rows, features), jnp.bfloat16),
            pltpu.VMEM((rows, tokens), jnp.float32),
            pltpu.VMEM((rows, tokens), jnp.float32),
            pltpu.SemaphoreType.DMA((2,)),
            pltpu.SemaphoreType.DMA((3,)),
            pltpu.SemaphoreType.DMA((2, n_dp, n_tensor)),
            pltpu.SemaphoreType.DMA((2, n_dp, 1 + n_lines)),
            pltpu.SemaphoreType.DMA((2, n_dp, n_lines)),
            pltpu.SemaphoreType.DMA((2,)),
        ],
        compiler_params=pltpu.CompilerParams(
            collective_id=0, has_side_effects=True, vmem_limit_bytes=56 * 2**20
        ),
        name="gather_forward",
    )(x, y, w_gate, w_up, w_down)

    wide = min(depth, 512)
    per_block = depth // wide
    whole = pl.BlockSpec((rows, tokens), lambda i: (0, 0))
    act_spec = pl.BlockSpec((None, tokens, wide), lambda i: (i // per_block, 0, i % per_block))
    out_spec = pl.BlockSpec((rows, wide), lambda i: (0, i))
    fisher = jax.ShapeDtypeStruct((rows, features), jnp.float32)
    return pl.pallas_call(
        functools.partial(squares, count, seq),
        grid=(features // wide,),
        out_shape=(fisher, fisher, fisher),
        in_specs=[whole, whole, whole, act_spec, act_spec],
        out_specs=(out_spec, out_spec, out_spec),
        compiler_params=pltpu.CompilerParams(vmem_limit_bytes=56 * 2**20),
        name="squares",
    )(gg, gu, hid, xb, yb)


def solution(mesh):
    n_dp, n_tensor = mesh.shape["dp"], mesh.shape["tensor"]
    return jax.shard_map(
        functools.partial(local, n_dp, n_tensor),
        mesh=mesh,
        in_specs=(
            P(("parts", "dp"), None, "tensor"),
            P(("parts", "dp"), None, "tensor"),
            P(("parts", "dp", "tensor"), None),
            P(("parts", "dp", "tensor"), None),
            P(("parts", "dp", "tensor"), None),
        ),
        out_specs=(
            P(("parts", "dp", "tensor"), None),
            P(("parts", "dp", "tensor"), None),
            P(("parts", "dp", "tensor"), None),
        ),
        check_vma=False,
    )
```

time: 384 us -> 106 us (0.28)
  matrix products: 183 us -> 0 us
  waiting for transfers between devices: 133 us -> 0 us
  Pallas kernels: 0 us -> 105 us
  other arithmetic: 32.2 us -> 0 us
  local copies, waits for them, and re-layouts: 20.9 us -> 0 us
  between operations: 13.8 us -> 0.64 us
    dot_general x24 -> x0, matrix products: 183 us -> none  [the longest x4 48.7 us: example_terms(): g_gate = jnp.dot(grad_gate, x_ex, preferred_element_type=jnp.float32)]
    all_gather x4 -> x0, waiting for transfers between devices: 132 us -> none  [the longest x1 35.9 us: local(): lax.all_gather(y_rows, 'tensor', axis=2, tiled=True)]
    pallas_call x0 -> x2, Pallas kernels: none -> 105 us  [the longest x1 62.5 us: local(): pl.pallas_call(functools.partial(gather_forward, n_dp, n_tensor), out_sha...]
    div x2 -> x0, other arithmetic: 32.2 us -> none  [local(): return (totals[0] / count, totals[1] / count, totals[2] / count)]
    while x56 -> x0, local copies, waits for them, and re-layouts: 20.9 us -> none
  transfers between devices with their start and end apart: 4 -> 0, of which waited for: 4 -> 0; matrix products, arithmetic and copies ran while one was open for 0% -> 0% of each run, Pallas kernels for 0% -> 0%
where the time goes in v1:
time: 106 us; the launch traced here: 105 us
  Pallas kernels  105 us (99%)
    pallas_call x1, Pallas kernels, local(): pl.pallas_call(functools.partial(gather_forward, n_dp, n_tensor), out_sha...  62.5 us
    pallas_call x1, Pallas kernels, local(): pl.pallas_call(functools.partial(squares, count, seq), grid=(features //...  42.1 us

profile of v1, /device:TPU:0, one launch (start us, length us, event | category | flops | bytes accessed | tf_op | source)
XLA Modules:
  0.0 105.2 jit_solution(5440991927391794365)
XLA Ops:
  0.6 62.5 %gather_forward.1 = (bf16[4,512,1024]{2,1,0:T(8,128)(2,1)}, bf16[4,512,1024]{2,1,0:T(8,128)(2,1)}, bf16[896,512]{1,0:T(8,128)(2,1)}, bf16[896,512]{1,0:T(8,128)(2,1)}, bf16[896,512]{1,0:T(8,128)(2,1)}) custom-call(bf16[128,1024]{1,0:T(8,128)(2,1)} %bitcast.2, bf16[128,1024]{1,0:T(8,128)(2,1)} %bitcast.3, bf16[896,4096]{1,0:T(8,128)(2,1)} %wg_ref.1, ...), custom_call_target="tpu_custom_call" | custom-call | tf_op jit(solution)/shard_map/gather_forward/pallas_call | solution.py:251
  63.1 42.1 %squares.1 = (f32[896,4096]{1,0:T(8,128)}, f32[896,4096]{1,0:T(8,128)}, f32[896,4096]{1,0:T(8,128)}) custom-call(bf16[896,512]{1,0:T(8,128)(2,1)} %get-tuple-element.8.gg_ref, bf16[896,512]{1,0:T(8,128)(2,1)} %get-tuple-element.9.gu_ref, bf16[896,512]{1,0:T(8,128)(2,1)} %get-tuple-element.10.hid_ref, bf16[4,512,1024]{2,1,0:T(8,128)(2,1)} %get-tuple-element.11.x_ref, ...), custom_call_target="tpu_custom_call" | custom-call | tf_op jit(solution)/shard_map/squares/pallas_call | solution.py:283

commit v2 on v1

--- a/solution.py
+++ b/solution.py
@@ -127,17 +127,16 @@
                 guarded(cond, lambda: arrived(a, safe, tt))
                 push(a, safe, tt, sib_sem.at[a, safe, tt // 2], {"tensor": sibling}, cond)
 
-    def from_sibling(a):
-        for zz in range(n_dp):
+    def from_sibling(a, first, number):
+        for i in range(number):
             for l in range(n_lines):
-                arrived(a, zz, 2 * l + 1 - core)
+                arrived(a, first + i, 2 * l + 1 - core)
 
     chunk = row_chunk(rows, 448)
 
     def project(w, act, acc, k):
-        @pl.loop(0, rows // chunk)
-        def _(i):
-            r = pl.ds(pl.multiple_of(i * chunk, chunk), chunk)
+        for i in range(rows // chunk):
+            r = slice(i * chunk, (i + 1) * chunk)
             part = lax.dot_general(
                 w[r, k * depth:(k + 1) * depth], act[k], NT,
                 preferred_element_type=jnp.float32,
@@ -160,7 +159,7 @@
         on_line(1, 0)
     from_peers(0, n_dp - 1)
     on_line(1, 1)
-    from_sibling(0)
+    from_sibling(0, 0, n_dp)
     x_out = pltpu.make_async_copy(xb, xo_ref, out_sem.at[0])
     x_out.start()
     weights[0].wait()
@@ -189,26 +188,36 @@
         gate[r, :] = u * sig * (1.0 + g * (1.0 - sig))
         up[r, :] = silu
 
+    weights[2].wait()
+    parts = 2 if n_dp % 2 == 0 and n_dp > 2 else 1
+    size = n_dp // parts
+
+    def backward(first):
+        span = pl.ds(pl.multiple_of(first * unit, unit), size * unit)
+        for i in range(rows // chunk):
+            r = slice(i * chunk, (i + 1) * chunk)
+            grad = lax.dot_general(
+                wd[r, :depth], yb[0, span, :], NT, preferred_element_type=jnp.float32
+            )
+            for k in range(1, n_tensor):
+                grad += lax.dot_general(
+                    wd[r, k * depth:(k + 1) * depth], yb[k, span, :], NT,
+                    preferred_element_type=jnp.float32,
+                )
+            gg_ref[r, span] = (grad * gate[r, span]).astype(jnp.bfloat16)
+            gu_ref[r, span] = (grad * up[r, span]).astype(jnp.bfloat16)
+
+    near = (z // size) * size
+    if parts == 2:
+        from_sibling(1, near, size)
+        backward(near)
     from_peers(1, n_dp - 2)
     from_peers(1, n_dp - 1)
-    from_sibling(1)
+    far = size - near if parts == 2 else near
+    from_sibling(1, far, size)
     y_out = pltpu.make_async_copy(yb, yo_ref, out_sem.at[1])
     y_out.start()
-    weights[2].wait()
-
-    width = n_tensor
-
-    @pl.loop(0, rows // chunk)
-    def _(i):
-        r = pl.ds(pl.multiple_of(i * chunk, chunk), chunk)
-        grad = lax.dot_general(wd[r, :depth], yb[0], NT, preferred_element_type=jnp.float32)
-        for k in range(1, width):
-            grad += lax.dot_general(
-                wd[r, k * depth:(k + 1) * depth], yb[k], NT,
-                preferred_element_type=jnp.float32,
-            )
-        gg_ref[r, :] = (grad * gate[r, :]).astype(jnp.bfloat16)
-        gu_ref[r, :] = (grad * up[r, :]).astype(jnp.bfloat16)
+    backward(far)
 
     for wait in sent:
         wait()
@@ -222,9 +231,8 @@
     wide = 256 if columns % 256 == 0 else columns
     for act, grads, out in ((x_ref, gg_ref, fg_ref), (x_ref, gu_ref, fu_ref), (y_ref, hid_ref, fd_ref)):
         for q in range(columns // wide):
-            @pl.loop(0, rows // chunk)
-            def _(i):
-                r = pl.ds(pl.multiple_of(i * chunk, chunk), chunk)
+            for i in range(rows // chunk):
+                r = slice(i * chunk, (i + 1) * chunk)
                 total = None
                 for e in range(count):
                     span = slice(e * seq, (e + 1) * seq)

time: 106 us -> 87.2 us (0.82)
  Pallas kernels: 105 us -> 85.4 us
    pallas_call x1, Pallas kernels: 42.1 us -> 27.8 us  [local(): pl.pallas_call(functools.partial(squares, count, seq), grid=(features //...]
    pallas_call x1, Pallas kernels: 62.5 us -> 57.5 us  [local(): pl.pallas_call(functools.partial(gather_forward, n_dp, n_tensor), out_sha...]
where the time goes in v2:
time: 87.2 us; the launch traced here: 86 us
  Pallas kernels  85.4 us (98%)
    pallas_call x1, Pallas kernels, local(): pl.pallas_call(functools.partial(gather_forward, n_dp, n_tensor), out_sha...  57.5 us
    pallas_call x1, Pallas kernels, local(): pl.pallas_call(functools.partial(squares, count, seq), grid=(features //...  27.8 us

profile of v2, /device:TPU:0, one launch (start us, length us, event | category | flops | bytes accessed | tf_op | source)
XLA Modules:
  0.0 86.0 jit_solution(15397066023810408849)
XLA Ops:
  0.6 57.5 %gather_forward.1 = (bf16[4,512,1024]{2,1,0:T(8,128)(2,1)}, bf16[4,512,1024]{2,1,0:T(8,128)(2,1)}, bf16[896,512]{1,0:T(8,128)(2,1)}, bf16[896,512]{1,0:T(8,128)(2,1)}, bf16[896,512]{1,0:T(8,128)(2,1)}) custom-call(bf16[128,1024]{1,0:T(8,128)(2,1)} %bitcast.2, bf16[128,1024]{1,0:T(8,128)(2,1)} %bitcast.3, bf16[896,4096]{1,0:T(8,128)(2,1)} %wg_ref.1, ...), custom_call_target="tpu_custom_call" | custom-call | tf_op jit(solution)/shard_map/gather_forward/pallas_call | solution.py:259
  58.2 27.8 %squares.1 = (f32[896,4096]{1,0:T(8,128)}, f32[896,4096]{1,0:T(8,128)}, f32[896,4096]{1,0:T(8,128)}) custom-call(bf16[896,512]{1,0:T(8,128)(2,1)} %get-tuple-element.8.gg_ref, bf16[896,512]{1,0:T(8,128)(2,1)} %get-tuple-element.9.gu_ref, bf16[896,512]{1,0:T(8,128)(2,1)} %get-tuple-element.10.hid_ref, bf16[4,512,1024]{2,1,0:T(8,128)(2,1)} %get-tuple-element.11.x_ref, ...), custom_call_target="tpu_custom_call" | custom-call | tf_op jit(solution)/shard_map/squares/pallas_call | solution.py:291

commit v3 on v2

--- a/solution.py
+++ b/solution.py
@@ -20,7 +20,7 @@
     x_ref, y_ref, wg_ref, wu_ref, wd_ref,
     xo_ref, yo_ref, gg_ref, gu_ref, hid_ref,
     xb, yb, wg, wu, wd, gate, up,
-    own_sem, w_sem, recv_sem, line_sem, sib_sem, out_sem,
+    own_sem, w_sem, recv_sem, line_sem, sib_sem, pair_sem, out_sem,
 ):
     z, t = lax.axis_index("dp"), lax.axis_index("tensor")
     core = lax.rem(t, 2)
@@ -69,6 +69,9 @@
         copy.wait()
 
     sent = []
+    paired = n_dp % 2 == 0
+    even = lax.rem(z, 2) == 0
+    partner = z + 1 - 2 * lax.rem(z, 2)
 
     def slot(a, zz, tt):
         return bufs[a].at[tt, pl.ds(zz * unit, unit), :]
@@ -114,7 +117,10 @@
             if sign <= 0:
                 push(a, safe, t, line_sem.at[a, safe, 1], {"dp": z - 1}, both(cond, has_down))
             for j in range(1, n_lines):
-                push(a, safe, t, line_sem.at[a, safe, 1 + j], {"tensor": peer(j)}, cond)
+                over = cond
+                if a == 1 and k == 1 and paired:
+                    over = both(cond, even if sign > 0 else jnp.logical_not(even))
+                push(a, safe, t, line_sem.at[a, safe, 1 + j], {"tensor": peer(j)}, over)
             push(a, safe, t, sib_sem.at[a, safe, line], {"tensor": sibling}, cond)
 
     def from_peers(a, k):
@@ -125,6 +131,8 @@
             for j in range(1, n_lines):
                 tt = peer(j)
                 guarded(cond, lambda: arrived(a, safe, tt))
+                if a == 1 and k == 0 and paired:
+                    push(a, safe, tt, pair_sem.at[j - 1], {"dp": partner}, None)
                 push(a, safe, tt, sib_sem.at[a, safe, tt // 2], {"tensor": sibling}, cond)
 
     def from_sibling(a, first, number):
@@ -274,6 +282,7 @@
             pltpu.SemaphoreType.DMA((2, n_dp, n_tensor)),
             pltpu.SemaphoreType.DMA((2, n_dp, 1 + n_lines)),
             pltpu.SemaphoreType.DMA((2, n_dp, n_lines)),
+            pltpu.SemaphoreType.DMA((n_lines,)),
             pltpu.SemaphoreType.DMA((2,)),
         ],
         compiler_params=pltpu.CompilerParams(

time: 87.2 us -> 91 us (1.044); the launches traced: 86 us -> 90.9 us
  Pallas kernels: 85.4 us -> 90.3 us
    pallas_call x1, Pallas kernels: 57.5 us -> 62.4 us  [local(): pl.pallas_call(functools.partial(gather_forward, n_dp, n_tensor), out_sha...]
where the time goes in v3:
time: 91 us; the launch traced here: 90.9 us
  Pallas kernels  90.3 us (99%)
    pallas_call x1, Pallas kernels, local(): pl.pallas_call(functools.partial(gather_forward, n_dp, n_tensor), out_sha...  62.4 us
    pallas_call x1, Pallas kernels, local(): pl.pallas_call(functools.partial(squares, count, seq), grid=(features //...  27.8 us

profile of v3, /device:TPU:0, one launch (start us, length us, event | category | flops | bytes accessed | tf_op | source)
XLA Modules:
  0.0 90.9 jit_solution(1011907497471827515)
XLA Ops:
  0.6 62.4 %gather_forward.1 = (bf16[4,512,1024]{2,1,0:T(8,128)(2,1)}, bf16[4,512,1024]{2,1,0:T(8,128)(2,1)}, bf16[896,512]{1,0:T(8,128)(2,1)}, bf16[896,512]{1,0:T(8,128)(2,1)}, bf16[896,512]{1,0:T(8,128)(2,1)}) custom-call(bf16[128,1024]{1,0:T(8,128)(2,1)} %bitcast.2, bf16[128,1024]{1,0:T(8,128)(2,1)} %bitcast.3, bf16[896,4096]{1,0:T(8,128)(2,1)} %wg_ref.1, ...), custom_call_target="tpu_custom_call" | custom-call | tf_op jit(solution)/shard_map/gather_forward/pallas_call | solution.py:267
  63.0 27.8 %squares.1 = (f32[896,4096]{1,0:T(8,128)}, f32[896,4096]{1,0:T(8,128)}, f32[896,4096]{1,0:T(8,128)}) custom-call(bf16[896,512]{1,0:T(8,128)(2,1)} %get-tuple-element.8.gg_ref, bf16[896,512]{1,0:T(8,128)(2,1)} %get-tuple-element.9.gu_ref, bf16[896,512]{1,0:T(8,128)(2,1)} %get-tuple-element.10.hid_ref, bf16[4,512,1024]{2,1,0:T(8,128)(2,1)} %get-tuple-element.11.x_ref, ...), custom_call_target="tpu_custom_call" | custom-call | tf_op jit(solution)/shard_map/squares/pallas_call | solution.py:300
